TPU v7x, 256 devices: a whole 4x4x8 slice. The times are simulated.
256 devices in a mesh: row: 16 (over y, x), col: 16 (over z, core).
Axes of the slice: x: 4, y: 4, z: 8, core: 2. Of those that a mesh axis runs over, the one named last changes fastest.
Arguments:
- matrix: bfloat16 [24576, 24576], P('row', 'col'), may hold values from -6 to 6
- inverses: bfloat16 [2, 256, 256], replicated, may hold values from -0.09 to 0.1, as said below
Outputs:
- factored: bfloat16 [24576, 24576], P('row', 'col')
- panels: bfloat16 [24576, 512], P('row')
Inputs may be any that keep to these rules, and one draw needn't show every extreme that they name: `inverses`: each of the two matrices is lower triangular with a diagonal between 0.05 and 0.1.
All inputs are finite; a program needn't handle non-finite values.
Results may differ from a plain program's by a relative error of at most 0.0057.
Values may be sent and summed in bfloat16 or wider, within the bound.
No kernel may reach another device: no remote copies, remote signals or barrier semaphores. Data moves between devices by JAX's collectives and lax.ppermute only.
A program may use at most 128 MiB of HBM per device.

v0:
```python
import jax
import jax.numpy as jnp
from jax import lax
from jax.sharding import PartitionSpec as P


def from_root(value, axis, source):
    kept = jnp.where(lax.axis_index(axis) == source, value, 0).astype(value.dtype)
    return lax.psum(kept, axis)


def outer_term(left_rows, right_rows):
    return lax.dot_general(
        left_rows, right_rows, (((1,), (1,)), ((), ())), preferred_element_type=jnp.float32
    )


def shards(matrix, inverses):
    width = inverses.shape[1]
    rows_local = matrix.shape[0]
    row_count = lax.axis_size("row")
    col_count = lax.axis_size("col")
    row_rank = lax.axis_index("row")
    col_rank = lax.axis_index("col")
    blocks_row = rows_local // width
    blocks_col = matrix.shape[1] // width
    ratio_blocks = col_count // row_count
    global_rows = jnp.repeat(jnp.arange(blocks_row, dtype=jnp.int32) * row_count + row_rank, width)
    source_row = col_rank % row_count
    source_slot = col_rank // row_count

    def factor(panel, inverse, start_block, owner_col):
        product = jnp.dot(panel, inverse.T, preferred_element_type=jnp.float32)
        masked = jnp.where((global_rows >= start_block)[:, None], product, 0.0).astype(jnp.bfloat16)
        return from_root(masked, "col", owner_col)

    def columns_of(left_rows):
        gathered = lax.all_gather(left_rows, "row", axis=0, tiled=True)
        gathered = gathered.reshape(row_count, blocks_col, ratio_blocks, width, width)
        mine = lax.dynamic_index_in_dim(gathered, source_row, 0, keepdims=False)
        mine = lax.dynamic_index_in_dim(mine, source_slot, 1, keepdims=False)
        return mine.reshape(blocks_col * width, width)

    first_rows = factor(matrix[:, :width], inverses[0], 1, 0)
    first_cols = columns_of(first_rows)
    partial_value = matrix.astype(jnp.float32) - outer_term(first_rows, first_cols)
    head = partial_value[:, :width].astype(jnp.bfloat16)
    second_rows = factor(head, inverses[1], 2, 1)
    second_cols = columns_of(second_rows)
    factored = (partial_value - outer_term(second_rows, second_cols)).astype(jnp.bfloat16)
    return (factored, jnp.concatenate([first_rows, second_rows], axis=1))


def solution(mesh):
    return jax.shard_map(
        shards,
        mesh=mesh,
        in_specs=(P("row", "col"), P()),
        out_specs=(P("row", "col"), P("row", None)),
        check_vma=False,
    )
```

profile of v0, /device:TPU:1, one launch (start us, length us, event | category | flops | bytes accessed | tf_op | source)
XLA Modules:
  0.0 456.7 jit_solution(4977230878266750554)
XLA Ops:
  7.2 0.0 all-reduce.3.cloned.1.call-start
  7.2 0.1 broadcast_in_dim.30
  7.3 2.5 fusion.4
  9.8 0.0 all-reduce.3.cloned.1.call-update
  9.8 0.0 all-gather.3.cloned.1.call-start
  9.9 115.4 %all-reduce.3.cloned.1.call-done = bf16[1536,256]{1,0:T(8,128)(2,1)} async-done(((bf16[1536,256]{1,0:T(8,128)(2,1)}), bf16[1536,256]{1,0:T(8,128)(2,1)}) %all-reduce.3.cloned.1.call-update) | async-done | bytes 786448 | tf_op jit(solution)/shard_map/psum | solution.py:9
  125.2 0.0 all-gather.3.cloned.1.call-update
  125.3 0.0 all-reduce.5.cloned.1.call-start
  125.3 0.1 broadcast_in_dim.34
  125.4 98.0 %all-gather.3.cloned.1.call-done = bf16[24576,256]{1,0:T(8,128)(2,1)} async-done(((bf16[1536,256]{1,0:T(8,128)(2,1)}), bf16[24576,256]{1,0:T(8,128)(2,1)}) %all-gather.3.cloned.1.call-update) | async-done | bytes 12582928 | tf_op jit(solution)/shard_map/all_gather | solution.py:38
  223.4 1.2 constant_dynamic-slice_fusion.1
  224.6 0.0 copy-start.3
  224.6 4.0 convolution_subtract_fusion.1
  228.6 0.0 copy-start
  228.7 3.5 copy-done
  232.2 0.0 copy-done.3
  232.2 0.0 copy-start.1
  232.2 1.3 fusion.3
  233.5 0.0 all-reduce.5.cloned.1.call-update
  233.5 0.0 all-gather.5.cloned.1.call-start
  233.6 110.4 %all-reduce.5.cloned.1.call-done = bf16[1536,256]{1,0:T(8,128)(2,1)} async-done(((bf16[1536,256]{1,0:T(8,128)(2,1)}), bf16[1536,256]{1,0:T(8,128)(2,1)}) %all-reduce.5.cloned.1.call-update) | async-done | bytes 786448 | tf_op jit(solution)/shard_map/psum | solution.py:9
  343.9 0.0 copy-start.2
  343.9 0.0 all-gather.5.cloned.1.call-update
  343.9 0.0 copy-done.1
  344.0 2.5 pad_maximum_fusion
  346.4 95.2 %all-gather.5.cloned.1.call-done = bf16[24576,256]{1,0:T(8,128)(2,1)} async-done(((bf16[1536,256]{1,0:T(8,128)(2,1)}), bf16[24576,256]{1,0:T(8,128)(2,1)}) %all-gather.5.cloned.1.call-update) | async-done | bytes 12582928 | tf_op jit(solution)/shard_map/all_gather | solution.py:38
  441.6 1.2 constant_dynamic-slice_fusion
  442.8 0.0 copy-done.2
  442.8 7.3 %fusion = bf16[1536,1536]{1,0:T(8,128)(2,1)} fusion(f32[1536,1536]{1,0:T(8,128)} %copy-done, bf16[1536,256]{1,0:T(8,128)(2,1)S(1)} %copy-done.2, bf16[1536,256]{1,0:T(8,128)(2,1)S(1)} %bitcast.15), kind=kOutput, calls=%fused_computation.2 | convolution fusion | flops 1212678144 | bytes 15728640 | tf_op jit(solution)/shard_map/dot_general | solution.py:13
  (3 shorter events, 0.0 us)
Async XLA Ops:
  7.2 118.1 %all-reduce.3.cloned.1.call-start = ((), (), s32[]{:S(2)}) async-start(), calls=%async_computation | async-start | bytes 1572864 | tf_op jit(solution)/shard_map/psum | solution.py:9
  9.8 213.6 %all-gather.3.cloned.1.call-start = ((), (), s32[]{:S(2)}) async-start(), calls=%async_computation.1 | async-start | bytes 13369344 | tf_op jit(solution)/shard_map/all_gather | solution.py:38
  125.3 218.7 %all-reduce.5.cloned.1.call-start = ((), (), s32[]{:S(2)}) async-start(), calls=%async_computation.2 | async-start | bytes 1572864 | tf_op jit(solution)/shard_map/psum | solution.py:9
  224.6 7.6 %copy-start.3 = (bf16[2,256,256]{2,1,0:T(8,128)(2,1)S(1)}, bf16[2,256,256]{2,1,0:T(8,128)(2,1)}, u32[]{:S(2)}) copy-start(bf16[2,256,256]{2,1,0:T(8,128)(2,1)} %param.3) | copy-start | bytes 786436
  228.6 3.5 copy-start
  232.2 111.8 %copy-start.1 = (bf16[1536,256]{1,0:T(8,128)(2,1)S(1)}, bf16[1536,256]{1,0:T(8,128)(2,1)}, u32[]{:S(2)}) copy-start(bf16[1536,256]{1,0:T(8,128)(2,1)} %all-reduce.3.cloned.1.call-done) | copy-start | bytes 2359300
  233.5 208.1 %all-gather.5.cloned.1.call-start = ((), (), s32[]{:S(2)}) async-start(), calls=%async_computation.3 | async-start | bytes 13369344 | tf_op jit(solution)/shard_map/all_gather | solution.py:38
  343.9 98.9 %copy-start.2 = (bf16[1536,256]{1,0:T(8,128)(2,1)S(1)}, bf16[1536,256]{1,0:T(8,128)(2,1)}, u32[]{:S(2)}) copy-start(bf16[1536,256]{1,0:T(8,128)(2,1)} %all-reduce.5.cloned.1.call-done) | copy-start | bytes 2359300
Sparse Core Ops, SparseCore 0:
  10.9 114.2 all-reduce.2
  128.0 95.3 all-gather.2
  233.6 110.2 all-reduce.4
  346.2 95.3 all-gather.4
where the time goes:
time: 457 us
  waiting for transfers between devices  419 us (92%)
  matrix products  15.1 us (3%)
  between operations  13.8 us (3%)
  local copies, waits for them, and re-layouts  6.09 us (1%)
    psum x2, waiting for transfers between devices, from_root(): return lax.psum(kept, axis)  226 us
    all_gather x2, waiting for transfers between devices, columns_of(): gathered = lax.all_gather(left_rows, 'row', axis=0, tiled=True)  193 us
    dot_general x2, matrix products, outer_term(): lax.dot_general(left_rows, right_rows, (((1,), (1,)), ((), ())), preferre...  11.3 us
  transfers between devices with their start and end apart: 4, of which 4 were waited for; matrix products, arithmetic and copies ran while one was open for 1% of the time, Pallas kernels for 0%

commit v1 on v0

--- a/solution.py
+++ b/solution.py
@@ -35,7 +35,12 @@
         return from_root(masked, "col", owner_col)
 
     def columns_of(left_rows):
-        gathered = lax.all_gather(left_rows, "row", axis=0, tiled=True)
+        row_list = []
+        many = lax.psum(1, "row")
+        for tick in tuple(range(left_rows.ndim)):
+            row_list.append(many if tick == 0 else 1)
+        low = jnp.tile(left_rows, row_list)
+        gathered = lax.all_to_all(low, "row", split_axis=0, concat_axis=0, tiled=True)
         gathered = gathered.reshape(row_count, blocks_col, ratio_blocks, width, width)
         mine = lax.dynamic_index_in_dim(gathered, source_row, 0, keepdims=False)
         mine = lax.dynamic_index_in_dim(mine, source_slot, 1, keepdims=False)

time: 457 us -> 665 us (1.46)
  waiting for transfers between devices: 419 us -> 596 us
  local copies, waits for them, and re-layouts: 6.09 us -> 19.8 us
  starting transfers between devices: 0.16 us -> 13.5 us
    all_to_all x0 -> x2, waiting for transfers between devices: none -> 369 us  [columns_of(): lax.all_to_all(low, 'row', split_axis=0, concat_axis=0, tiled=True)]
    all_gather x2 -> x0, waiting for transfers between devices: 193 us -> none  [columns_of(): gathered = lax.all_gather(left_rows, 'row', axis=0, tiled=True)]
    another operation x0 -> x2, local copies, waits for them, and re-layouts: none -> 13.6 us  [columns_of(): low = jnp.tile(left_rows, row_list)]
    all_to_all x0 -> x2, starting transfers between devices: none -> 13.4 us  [columns_of(): lax.all_to_all(low, 'row', split_axis=0, concat_axis=0, tiled=True)]
  transfers between devices with their start and end apart: 4 -> 4, of which waited for: 4 -> 4; matrix products, arithmetic and copies ran while one was open for 1% -> 0% of each run, Pallas kernels for 0% -> 0%
where the time goes in v1:
time: 665 us; the launch traced here: 660 us
  waiting for transfers between devices  596 us (90%)
  local copies, waits for them, and re-layouts  19.8 us (3%)
  matrix products  14.9 us (2%)
  between operations  14.1 us (2%)
  starting transfers between devices  13.5 us (2%)
    all_to_all x2, waiting for transfers between devices, columns_of(): lax.all_to_all(low, 'row', split_axis=0, concat_axis=0, tiled=True)  369 us
    psum x2, waiting for transfers between devices, from_root(): return lax.psum(kept, axis)  227 us
    another operation x2, local copies, waits for them, and re-layouts, columns_of(): low = jnp.tile(left_rows, row_list)  13.6 us
    all_to_all x2, starting transfers between devices, columns_of(): lax.all_to_all(low, 'row', split_axis=0, concat_axis=0, tiled=True)  13.4 us
  transfers between devices with their start and end apart: 4, of which 4 were waited for; matrix products, arithmetic and copies ran while one was open for 0% of the time, Pallas kernels for 0%

profile of v1, /device:TPU:1, one launch (start us, length us, event | category | flops | bytes accessed | tf_op | source)
XLA Modules:
  0.0 659.8 jit_solution(13167815841436633145)
XLA Ops:
  7.2 0.0 all-reduce.3.cloned.1.call-start
  7.2 0.1 broadcast_in_dim.30
  7.3 2.5 fusion.4
  9.8 0.0 all-reduce.3.cloned.1.call-update
  9.8 115.4 %all-reduce.3.cloned.1.call-done = bf16[1536,256]{1,0:T(8,128)(2,1)} async-done(((bf16[1536,256]{1,0:T(8,128)(2,1)}), bf16[1536,256]{1,0:T(8,128)(2,1)}) %all-reduce.3.cloned.1.call-update) | async-done | bytes 786448 | tf_op jit(solution)/shard_map/psum | solution.py:9
  125.2 6.8 %tile.4 = bf16[16,1536,256]{2,1,0:T(8,128)(2,1)} broadcast(bf16[1536,256]{1,0:T(8,128)(2,1)} %all-reduce.3.cloned.1.call-done), dimensions={1,2} | broadcast | bytes 13369344 | tf_op jit(solution)/shard_map/tile | solution.py:42
  132.1 0.0 copy-start.1
  132.1 6.7 %all-to-all-start = ((bf16[16,1536,256]{2,1,0:T(8,128)(2,1)}), bf16[16,1536,256]{2,1,0:T(8,128)(2,1)}, u32[]{:S(2)}, u32[]{:S(2)}) async-start(bf16[16,1536,256]{2,1,0:T(8,128)(2,1)} %tile.4), calls=%async_computation | async-start | bytes 25165824 | tf_op jit(solution)/shard_map/all_to_all | solution.py:43
  138.8 0.0 all-reduce.5.cloned.1.call-start
  138.8 0.1 broadcast_in_dim.34
  138.9 185.2 %all-to-all-done = bf16[16,1536,256]{2,1,0:T(8,128)(2,1)} async-done(((bf16[16,1536,256]{2,1,0:T(8,128)(2,1)}), bf16[16,1536,256]{2,1,0:T(8,128)(2,1)}, u32[]{:S(2)}, u32[]{:S(2)}) %all-to-all-start) | async-done | bytes 12582944 | tf_op jit(solution)/shard_map/all_to_all | solution.py:43
  324.1 1.2 constant_dynamic-slice_fusion.1
  325.3 0.0 copy-done.1
  325.3 0.0 copy-start.3
  325.3 3.8 convolution_subtract_fusion.1
  329.1 0.0 copy-start
  329.1 3.6 copy-done
  332.7 0.0 copy-done.3
  332.7 1.3 fusion.3
  334.0 0.0 all-reduce.5.cloned.1.call-update
  334.0 111.6 %all-reduce.5.cloned.1.call-done = bf16[1536,256]{1,0:T(8,128)(2,1)} async-done(((bf16[1536,256]{1,0:T(8,128)(2,1)}), bf16[1536,256]{1,0:T(8,128)(2,1)}) %all-reduce.5.cloned.1.call-update) | async-done | bytes 786448 | tf_op jit(solution)/shard_map/psum | solution.py:9
  445.6 6.8 %tile.5 = bf16[16,1536,256]{2,1,0:T(8,128)(2,1)} broadcast(bf16[1536,256]{1,0:T(8,128)(2,1)} %all-reduce.5.cloned.1.call-done), dimensions={1,2} | broadcast | bytes 13369344 | tf_op jit(solution)/shard_map/tile | solution.py:42
  452.4 0.0 copy-start.2
  452.4 6.7 %all-to-all-start.1 = ((bf16[16,1536,256]{2,1,0:T(8,128)(2,1)}), bf16[16,1536,256]{2,1,0:T(8,128)(2,1)}, u32[]{:S(2)}, u32[]{:S(2)}) async-start(bf16[16,1536,256]{2,1,0:T(8,128)(2,1)} %tile.5), calls=%async_computation.1 | async-start | bytes 25165824 | tf_op jit(solution)/shard_map/all_to_all | solution.py:43
  459.1 0.0 copy-done.2
  459.1 1.3 pad_maximum_fusion
  460.4 184.0 %all-to-all-done.1 = bf16[16,1536,256]{2,1,0:T(8,128)(2,1)} async-done(((bf16[16,1536,256]{2,1,0:T(8,128)(2,1)}), bf16[16,1536,256]{2,1,0:T(8,128)(2,1)}, u32[]{:S(2)}, u32[]{:S(2)}) %all-to-all-start.1) | async-done | bytes 12582944 | tf_op jit(solution)/shard_map/all_to_all | solution.py:43
  644.4 1.2 constant_dynamic-slice_fusion
  645.6 7.3 %fusion = bf16[1536,1536]{1,0:T(8,128)(2,1)} fusion(f32[1536,1536]{1,0:T(8,128)} %copy-done, bf16[1536,256]{1,0:T(8,128)(2,1)S(1)} %copy-done.2, bf16[1536,256]{1,0:T(8,128)(2,1)S(1)} %bitcast.15), kind=kOutput, calls=%fused_computation.2 | convolution fusion | flops 1212678144 | bytes 15728640 | tf_op jit(solution)/shard_map/dot_general | solution.py:13
  (3 shorter events, 0.0 us)
Async XLA Ops:
  7.2 118.1 %all-reduce.3.cloned.1.call-start = ((), (), s32[]{:S(2)}) async-start(), calls=%async_computation.2 | async-start | bytes 1572864 | tf_op jit(solution)/shard_map/psum | solution.py:9
  132.1 193.2 %copy-start.1 = (bf16[1536,256]{1,0:T(8,128)(2,1)S(1)}, bf16[1536,256]{1,0:T(8,128)(2,1)}, u32[]{:S(2)}) copy-start(bf16[1536,256]{1,0:T(8,128)(2,1)} %all-reduce.3.cloned.1.call-done) | copy-start | bytes 2359300
  132.1 192.0 %all-to-all-start = ((bf16[16,1536,256]{2,1,0:T(8,128)(2,1)}), bf16[16,1536,256]{2,1,0:T(8,128)(2,1)}, u32[]{:S(2)}, u32[]{:S(2)}) async-start(bf16[16,1536,256]{2,1,0:T(8,128)(2,1)} %tile.4), calls=%async_computation | async-start | bytes 25165824 | tf_op jit(solution)/shard_map/all_to_all | solution.py:43
  138.8 306.8 %all-reduce.5.cloned.1.call-start = ((), (), s32[]{:S(2)}) async-start(), calls=%async_computation.3 | async-start | bytes 1572864 | tf_op jit(solution)/shard_map/psum | solution.py:9
  325.3 7.4 %copy-start.3 = (bf16[2,256,256]{2,1,0:T(8,128)(2,1)S(1)}, bf16[2,256,256]{2,1,0:T(8,128)(2,1)}, u32[]{:S(2)}) copy-start(bf16[2,256,256]{2,1,0:T(8,128)(2,1)} %param.3) | copy-start | bytes 786436
  329.1 3.6 copy-start
  452.4 6.7 %copy-start.2 = (bf16[1536,256]{1,0:T(8,128)(2,1)S(1)}, bf16[1536,256]{1,0:T(8,128)(2,1)}, u32[]{:S(2)}) copy-start(bf16[1536,256]{1,0:T(8,128)(2,1)} %all-reduce.5.cloned.1.call-done) | copy-start | bytes 2359300
  452.4 192.0 %all-to-all-start.1 = ((bf16[16,1536,256]{2,1,0:T(8,128)(2,1)}), bf16[16,1536,256]{2,1,0:T(8,128)(2,1)}, u32[]{:S(2)}, u32[]{:S(2)}) async-start(bf16[16,1536,256]{2,1,0:T(8,128)(2,1)} %tile.5), calls=%async_computation.1 | async-start | bytes 25165824 | tf_op jit(solution)/shard_map/all_to_all | solution.py:43
Sparse Core Ops, SparseCore 0:
  10.9 114.2 all-reduce.2
  334.1 111.4 all-reduce.4
